TPU v7x, 256 devices: a whole 4x4x8 slice. The times are simulated.
256 devices in a mesh: row: 32 (over z_lo, x, core), col: 8 (over y, z_hi).
Axes of the slice: x: 4, y: 4, z: 8 (z_hi: 2, z_lo: 4; z = z_hi * 4 + z_lo), core: 2. Of those that a mesh axis runs over, the one named last changes fastest.
Arguments:
- c_panel: float32 [16384, 128], P('row', 'col'), may hold values from -0.046875 to 0.046875
- cbar_in: float32 [16384, 128], P('row', 'col'), may hold values from -6 to 6
- factor_diagonal_block: float32 [128, 128], replicated, may hold values from -0.9 to 4, as said below
- dbar_in: float32 [128, 128], replicated, may hold values from -6 to 6
- r_panel: float32 [128, 16384], P('row', 'col'), may hold values from -0.6 to 0.6
- rbar_in: float32 [128, 16384], P('row', 'col'), may hold values from -6 to 6
- b_block: float32 [16384, 16384], P('row', 'col'), may hold values from -0.046875 to 0.046875
- bbar_in: float32 [16384, 16384], P('row', 'col'), may hold values from -6 to 6
Outputs:
- cbar_out: float32 [16384, 128], P('row', 'col')
- bbar_out: float32 [16384, 16384], P('row', 'col')
- kernel_diagonal_adjoint: float32 [128, 128], P('row', 'col')
- rbar_out: float32 [128, 16384], P('row', 'col')
Inputs may be any that keep to these rules, and one draw needn't show every extreme that they name: factor_diagonal_block is lower triangular; its diagonal entries lie in 2 to 4 and its entries below the diagonal in -0.9 to 0.9.
All inputs are finite; a program needn't handle non-finite values.
Results may differ from a plain program's by a relative error of at most 0.00007.
Values sent between devices are 32-bit elements; how exact they have to be, the bound alone decides.
A program may use at most 64 MiB of HBM per device.

v0:
```python
import jax
import jax.numpy as jnp
from jax import lax
from jax.sharding import PartitionSpec as P


def lower_half_term(matrix):
    return jnp.tril(matrix) - 0.5 * jnp.diag(jnp.diag(matrix))


def body(c_panel, cbar_in, factor_diagonal_block, dbar_in, r_panel, rbar_in, b_block, bbar_in):
    highest = lax.Precision.HIGHEST
    col_width = c_panel.shape[1]
    row_height = r_panel.shape[0]
    col_index = lax.axis_index("col")
    row_index = lax.axis_index("row")
    column_adjoint_whole, c_full = (
        lax.all_gather(cbar_in, "col", axis=1, tiled=True),
        lax.all_gather(c_panel, "col", axis=1, tiled=True),
    )
    cbar_new = jax.scipy.linalg.solve_triangular(
        factor_diagonal_block, column_adjoint_whole.T, lower=True, trans="T"
    ).T
    product = jnp.dot(cbar_new.T, c_full, precision=highest, preferred_element_type=jnp.float32)
    product = lax.psum(product, "row")
    cbar_out = lax.dynamic_slice_in_dim(cbar_new, col_index * col_width, col_width, 1)
    r_full = lax.all_gather(r_panel, "row", axis=0, tiled=True)
    bbar_out = bbar_in - jnp.dot(
        cbar_new, r_full, precision=highest, preferred_element_type=jnp.float32
    )
    diagonal_adjoint_middle = dbar_in - jnp.tril(product)
    proj = lower_half_term(
        jnp.dot(
            factor_diagonal_block.T,
            diagonal_adjoint_middle,
            precision=highest,
            preferred_element_type=jnp.float32,
        )
    )
    left_product_term = jax.scipy.linalg.solve_triangular(
        factor_diagonal_block, proj, lower=True, trans="T"
    )
    sandwich_product = jax.scipy.linalg.solve_triangular(
        factor_diagonal_block, left_product_term.T, lower=True, trans="T"
    ).T
    diagonal_adjoint_whole = lower_half_term(sandwich_product + sandwich_product.T)
    dbar_rows = lax.dynamic_slice_in_dim(
        diagonal_adjoint_whole, row_index * row_height, row_height, 0
    )
    kernel_diagonal_adjoint = lax.dynamic_slice_in_dim(
        dbar_rows, col_index * col_width, col_width, 1
    )
    trailing_full = lax.dot_general(
        cbar_new,
        b_block,
        (((0,), (0,)), ((), ())),
        precision=highest,
        preferred_element_type=jnp.float32,
    )
    summed = lax.psum_scatter(trailing_full, "row", scatter_dimension=0, tiled=True)
    sym_full = diagonal_adjoint_whole + diagonal_adjoint_whole.T
    sym_rows = lax.dynamic_slice_in_dim(sym_full, row_index * row_height, row_height, 0)
    rbar_out = (
        rbar_in
        - summed
        - jnp.dot(sym_rows, r_full, precision=highest, preferred_element_type=jnp.float32)
    )
    return (cbar_out, bbar_out, kernel_diagonal_adjoint, rbar_out)


def solution(mesh):
    in_specs = (
        P("row", "col"),
        P("row", "col"),
        P(),
        P(),
        P("row", "col"),
        P("row", "col"),
        P("row", "col"),
        P("row", "col"),
    )
    out_specs = (P("row", "col"), P("row", "col"), P("row", "col"), P("row", "col"))
    return jax.shard_map(body, mesh=mesh, in_specs=in_specs, out_specs=out_specs, check_vma=False)
```

profile of v0, /device:TPU:1, one launch (start us, length us, event | category | flops | bytes accessed | tf_op | source)
XLA Modules:
  0.0 470.0 jit_solution(9765408951004738953)
XLA Ops:
  7.2 0.0 all-reduce.4.cloned.1.call-start
  7.2 0.9 select_bitcast_fusion
  8.1 9.8 %custom-call.7 = f32[1,128,128]{1,2,0:T(8,128)S(1)} custom-call(f32[1,128,128]{2,1,0:T(8,128)S(1)} %select_bitcast_fusion), custom_call_target="InvertDiagBlocksLowerTriangular" | custom-call | tf_op jit(solution)/shard_map/jit(_solve_triangular)/triangular_solve | solution.py:21
  17.9 0.0 copy-start.3
  17.9 41.7 %all_gather.11 = f32[512,128]{0,1:T(8,128)S(1)} all-gather(f32[512,16]{0,1:T(8,128)} %param.10), channel_id=1, replica_groups=mesh['row'=32,'col'=8] {'col'}, dimensions={1}, use_global_device_ids=true | all-gather | bytes 294912 | tf_op jit(solution)/shard_map/all_gather | solution.py:19
  59.6 0.0 copy-start
  59.6 0.0 copy-start.1
  59.6 38.9 %all_gather.9 = f32[512,128]{0,1:T(8,128)S(1)} all-gather(f32[512,16]{0,1:T(8,128)} %param.11), channel_id=1, replica_groups=mesh['row'=32,'col'=8] {'col'}, dimensions={1}, use_global_device_ids=true | all-gather | bytes 294912 | tf_op jit(solution)/shard_map/all_gather | solution.py:18
  98.5 0.4 fusion.3
  98.8 1.0 fusion.20
  99.8 5.5 %fusion.21 = f32[128,2048]{1,0:T(8,128)} fusion(f32[128,512]{1,0:T(8,128)S(1)} %fusion.3, f32[512,2048]{1,0:T(8,128)} %param.16), kind=kOutput, calls=%fused_computation.36 | convolution fusion | flops 1610612736 | bytes 5505024 | tf_op jit(solution)/shard_map/dot_general | solution.py:53
  105.3 0.0 all-reduce.4.cloned.1.call-update
  105.4 0.0 all-gather.3.cloned.1.call-start
  105.4 0.7 all-gather.3.cloned.1.call-update
  106.1 0.0 copy-done.3
  106.1 0.6 dynamic-slice.4
  107.4 0.6 dynamic-slice_bitcast_fusion
  108.0 283.4 %all-reduce.4.cloned.1.call-done = (f32[128,128]{1,0:T(8,128)}, f32[128,2048]{1,0:T(8,128)}) async-done(((f32[128,128]{1,0:T(8,128)}, f32[128,2048]{1,0:T(8,128)}), (f32[128,128]{1,0:T(8,128)}, f32[128,2048]{1,0:T(8,128)})) %all-reduce.4.cloned.1.call-update) | async-done | bytes 1114128 | tf_op jit(solution)/shard_map/psum | solution.py:25
  391.4 0.0 copy-done
  391.4 0.0 copy-done.1
  391.4 1.1 convolution_bitcast_fusion.1
  392.6 1.2 gather_fusion
  393.8 0.3 convolution_bitcast_fusion
  394.1 0.3 fusion.1
  394.4 0.1 copy.19
  394.5 1.2 gather_fusion.1
  395.8 0.1 multiply_subtract_fusion
  395.8 0.1 copy.20
  395.9 0.7 dynamic_slice.11
  396.6 56.3 %all-gather.3.cloned.1.call-done = f32[32,4,2048]{2,1,0:T(4,128)} async-done(((f32[1,4,2048]{2,1,0:T(4,128)}), f32[32,4,2048]{2,1,0:T(4,128)}) %all-gather.3.cloned.1.call-update) | async-done | bytes 1048592 | tf_op jit(solution)/shard_map/all_gather | solution.py:27
  452.9 1.6 reshape.30
  454.5 0.0 copy-start.2
  454.5 6.6 %convolution_subtract_fusion = f32[512,2048]{1,0:T(8,128)} fusion(f32[512,2048]{1,0:T(8,128)} %param.17, f32[128,512]{1,0:T(8,128)S(1)} %fusion.3, f32[128,2048]{1,0:T(8,128)S(1)} %reshape.30), kind=kOutput, calls=%fused_computation.2 | convolution fusion | flops 1611661312 | bytes 9699328 | tf_op jit(solution)/shard_map/dot_general | solution.py:28
  461.1 0.0 copy-done.2
  461.1 2.1 convolution_subtract_fusion.1
  (2 shorter events, 0.0 us)
Async XLA Ops:
  7.2 384.3 %all-reduce.4.cloned.1.call-start = ((), (), s32[]{:S(2)}) async-start(), calls=%async_computation.1 | async-start | bytes 2228224 | tf_op jit(solution)/shard_map/psum | solution.py:25
  17.9 88.2 %copy-start.3 = (u32[256]{0:T(256)S(1)}, u32[256]{0:T(256)}, u32[]{:S(2)}) copy-start(u32[256]{0:T(256)} %constant.89) | copy-start | bytes 3076
  59.6 331.9 %copy-start = (f32[128,128]{1,0:T(8,128)S(1)}, f32[128,128]{1,0:T(8,128)}, u32[]{:S(2)}) copy-start(f32[128,128]{1,0:T(8,128)} %param.12) | copy-start | bytes 196612
  59.6 331.9 %copy-start.1 = (f32[128,128]{1,0:T(8,128)S(1)}, f32[128,128]{1,0:T(8,128)}, u32[]{:S(2)}) copy-start(f32[128,128]{1,0:T(8,128)} %param.13) | copy-start | bytes 196612
  105.4 347.5 %all-gather.3.cloned.1.call-start = ((), (), s32[]{:S(2)}) async-start(), calls=%async_computation | async-start | bytes 1081344 | tf_op jit(solution)/shard_map/all_gather | solution.py:27
  454.5 6.6 %copy-start.2 = (f32[4,2048]{1,0:T(4,128)S(1)}, f32[4,2048]{1,0:T(4,128)}, u32[]{:S(2)}) copy-start(f32[4,2048]{1,0:T(4,128)} %param.15) | copy-start | bytes 98308
Sparse Core Ops, SparseCore 0:
  105.5 285.9 all-reduce.3
  393.4 59.3 all-gather.2
where the time goes:
time: 470 us
  waiting for transfers between devices  340 us (72%)
  blocking collectives  80.6 us (17%)
  matrix products  17.2 us (4%)
  between operations  14.8 us (3%)
  other arithmetic  10.8 us (2%)
  local copies, waits for them, and re-layouts  6.14 us (1%)
    psum x1, waiting for transfers between devices, body(): product = lax.psum(product, 'row')  283 us
    all_gather x1, waiting for transfers between devices, body(): r_full = lax.all_gather(r_panel, 'row', axis=0, tiled=True)  56.3 us
    all_gather x1, blocking collectives, body(): lax.all_gather(c_panel, 'col', axis=1, tiled=True)  41.7 us
    all_gather x1, blocking collectives, body(): lax.all_gather(cbar_in, 'col', axis=1, tiled=True)  38.9 us
    another operation x2, other arithmetic, body(): jax.scipy.linalg.solve_triangular(factor_diagonal_block, column_adjoint_w...  10.7 us
  transfers between devices with their start and end apart: 2, of which 2 were waited for; matrix products, arithmetic and copies ran while one was open for 1% of the time, Pallas kernels for 0%

commit v1 on v0

v1 whole, which is shorter than its diff:
```python
import functools

import jax
import jax.numpy as jnp
from jax import lax
from jax.experimental import pallas as pl
from jax.experimental.pallas import tpu as pltpu
from jax.sharding import PartitionSpec as P

F32 = jnp.float32
BF16 = jnp.bfloat16
HI = lax.Precision.HIGHEST
MESH = pl.DeviceIdType.MESH
ANY = pl.ANY
NX, NZ, NY, NC, NH = 4, 4, 4, 2, 2
CH = 4
CW = 512


def dot(a, b, contract=((1,), (0,)), precision=HI):
    return lax.dot_general(
        a, b, (contract, ((), ())), precision=precision, preferred_element_type=F32
    )


def split(a):
    high = a.astype(BF16)
    return high, (a - high.astype(F32)).astype(BF16)


def kernel(
    c_hbm, cbar_hbm, l_hbm, d_hbm, r_hbm, rbar_hbm, b_hbm, bbar_hbm,
    cbar_out, bbar_out, kda_out, rbar_out,
    l_v, d_v, c_v, rbar_v, b_v, bbar_v, bh_v, bl_v,
    cg, rg, w_v, wp_v, x3_v, rh_v, rl_v,
    tb, tc, ts, xo, xd, xs, xa, zs, zr,
    ms, ma, mt, mb, mg,
    co_v, kd_v, ro_v,
    lsem, bsem, osem,
    cgs, cgr, rs, rr, tss, trs, xss, xrs, zss, zrs, mss, mrs,
):
    row, col = lax.axis_index("row"), lax.axis_index("col")
    core, x, zl = row % NC, (row // NC) % NX, row // (NC * NX)
    y, zh = col // NH, col % NH

    def dev(dz=0, dx=0, fc=0, dy=0, fz=0):
        c2 = 1 - core if fc else core
        h2 = 1 - zh if fz else zh
        z2, x2, y2 = (zl + dz) % NZ, (x + dx) % NX, (y + dy) % NY
        return (z2 * (NX * NC) + x2 * NC + c2, y2 * NH + h2)

    xc = [(dx, fc) for dx in range(NX) for fc in range(NC)][1:]
    zz = [(dz, fz) for dz in range(NZ) for fz in range(NH)][1:]
    peers = [dev(dx=dx, fc=fc) for dx, fc in xc]
    peers += [dev(dz=dz, fz=fz) for dz, fz in zz]
    peers += [dev(dy=dy) for dy in range(1, NY)]

    barrier = pltpu.get_barrier_semaphore()
    for peer in peers:
        pl.semaphore_signal(barrier, inc=1, device_id=peer, device_id_type=MESH)

    def local(src, dst, sem):
        copy = pltpu.make_async_copy(src, dst, sem)
        copy.start()
        return copy

    sent = []

    def send(src, dst, ssem, rsem, to):
        copy = pltpu.make_async_remote_copy(
            src_ref=src, dst_ref=dst, send_sem=ssem, recv_sem=rsem,
            device_id=to, device_id_type=MESH,
        )
        copy.start()
        sent.append(copy)
        return copy

    my_slot = core * (NX * NZ) + x * NZ + zl
    l_c = local(l_hbm, l_v, lsem.at[0])
    cg_c = local(cbar_hbm, cg.at[col], lsem.at[1])
    c_c = local(c_hbm, c_v, lsem.at[2])
    r_c = local(r_hbm, rg.at[my_slot], lsem.at[3])
    d_c = local(d_hbm, d_v, lsem.at[4])
    rb_c = local(rbar_hbm, rbar_v, lsem.at[5])
    b_c = [
        local(b_hbm.at[:, pl.ds(k * CW, CW)], b_v.at[:, pl.ds(k * CW, CW)], bsem.at[k])
        for k in range(CH)
    ]
    bb_c = local(bbar_hbm, bbar_v, lsem.at[6])

    pl.semaphore_wait(barrier, len(peers))

    mine = cg.at[col]
    cz = send(cbar_hbm, mine, cgs.at[0], cgr.at[0], dev(fz=1))
    cy = [
        send(cbar_hbm, mine, cgs.at[dy], cgr.at[dy], dev(dy=dy)) for dy in range(1, NY)
    ]
    rz = [
        send(r_hbm, rg.at[my_slot], rs.at[dz - 1], rr.at[dz - 1], dev(dz=dz))
        for dz in range(1, NZ)
    ]

    rows = lax.broadcasted_iota(jnp.int32, (128, 128), 0)
    cols = lax.broadcasted_iota(jnp.int32, (128, 128), 1)
    l_c.wait()
    u = l_v[...].T
    eye = rows == cols
    w = jnp.where(eye, 1.0 / jnp.where(eye, u, 1.0), 0.0)

    def level(w, s):
        mask = (rows // (2 * s) == cols // (2 * s)) & (rows % (2 * s) < s) & (cols % (2 * s) >= s)
        return w - dot(dot(w, jnp.where(mask, u, 0.0)), w)

    for s in (1, 2, 4):
        w = level(w, s)

    cz.wait_recv()
    part = cg.at[y * NH + 1 - zh]
    cy += [
        send(part, part, cgs.at[3 + dy], cgr.at[3 + dy], dev(dy=dy)) for dy in range(1, NY)
    ]

    for copy in rz:
        copy.wait_recv()
    r_c.wait()

    def group(g):
        return rg.at[pl.ds(core * (NX * NZ) + ((x + g) % NX) * NZ, NZ)]

    own = group(0)
    r_right = send(own, own, rs.at[3], rr.at[3], dev(dx=1))
    r_left = send(own, own, rs.at[4], rr.at[4], dev(dx=3))
    r_core = [send(own, own, rs.at[5], rr.at[5], dev(fc=1))]

    for s in (8, 16, 32, 64):
        w = level(w, s)
    w_v[...] = w
    natural = (rows % 16) // 4 * 32 + (rows // 16) % 4 * 8 + rows // 64 * 4 + rows % 4
    wp = dot(jnp.where(cols == natural, 1.0, 0.0), w)
    wp_v[...] = wp

    for k in range(CH):
        b_c[k].wait()
        high, low = split(b_v[:, k * CW : (k + 1) * CW])
        bh_v[:, k * CW : (k + 1) * CW] = high
        bl_v[:, k * CW : (k + 1) * CW] = low

    for copy in cy:
        copy.wait_recv()
    cg_c.wait()
    ct = cg[...].reshape(128, 512)

    c_c.wait()
    ms[...] = dot(c_v[...], ct, ((1,), (1,)))
    m_x = [
        send(ms, ma.at[i], mss.at[i], mrs.at[i], dev(dx=dx, fc=fc))
        for i, (dx, fc) in enumerate(xc)
    ]

    ctn = dot(wp, ct)
    nh, nl = split(ctn)
    both = jnp.concatenate([nh, nl], axis=0)

    def chunk(k):
        where = slice(k * CW, (k + 1) * CW)
        p = dot(both, bh_v[:, where], precision=None)
        t = p[:128] + p[128:] + dot(nh, bl_v[:, where], precision=None)
        tb[k, 0] = t[:64]
        tb[k, 1] = t[64:]
        return send(tb.at[k, 1 - core], tc.at[k], tss.at[k], trs.at[k], dev(fc=1))

    t_core = []
    x_opp = []
    x_dir = []
    x_acc = []

    def after_core(k):
        t_core[k].wait_recv()
        v = tb[k, core] + tc[k]
        for q in range(NX):
            ts[k, q] = v[16 * q : 16 * (q + 1)]
        step = 1 if k % 2 == 0 else 3
        x_opp.append(
            send(ts.at[k, (x + 2) % NX], xo.at[k], xss.at[k, 0], xrs.at[k, 0], dev(dx=step))
        )
        x_dir.append(
            send(ts.at[k, (x - step + NX) % NX], xd.at[k], xss.at[k, 1], xrs.at[k, 1], dev(dx=4 - step))
        )

    t_core.append(chunk(0))

    total = ms[...]
    for i, copy in enumerate(m_x):
        copy.wait_recv()
        total = total + ma[i]
    mt[...] = total
    m_z = [
        send(mt, mb.at[i], mss.at[7 + i], mrs.at[7 + i], dev(dz=dz, fz=fz))
        for i, (dz, fz) in enumerate(zz)
    ]

    t_core.append(chunk(1))
    after_core(0)
    t_core.append(chunk(2))
    after_core(1)
    t_core.append(chunk(3))
    after_core(2)
    after_core(3)

    r_right.wait_recv()
    r_left.wait_recv()
    from_left, from_right = group(3), group(1)
    half_a = from_left.at[:, :, pl.ds(0, 1024)]
    half_b = from_right.at[:, :, pl.ds(1024, 1024)]
    r_fa = send(half_a, half_a, rs.at[6], rr.at[6], dev(dx=1))
    r_fb = send(half_b, half_b, rs.at[7], rr.at[7], dev(dx=3))
    r_core.append(send(from_left, from_left, rs.at[8], rr.at[8], dev(fc=1)))
    r_core.append(send(from_right, from_right, rs.at[9], rr.at[9], dev(fc=1)))

    for k in range(CH):
        step = 1 if k % 2 == 0 else 3
        x_opp[k].wait_recv()
        xs[k] = ts[k, (x + step) % NX] + xo[k]
        x_acc.append(send(xs.at[k], xa.at[k], xss.at[k, 2], xrs.at[k, 2], dev(dx=step)))

    same, other = mt[...], None
    for i, (dz, fz) in enumerate(zz):
        m_z[i].wait_recv()
        if fz:
            other = mb[i] if other is None else other + mb[i]
        else:
            same = same + mb[i]
    mg[col] = same
    mg[y * NH + 1 - zh] = other
    pair = mg.at[pl.ds(y * NH, NH)]
    m_y = [
        send(pair, pair, mss.at[13 + dy], mrs.at[13 + dy], dev(dy=dy)) for dy in range(1, NY)
    ]

    co_v[...] = dot(w_v[pl.ds(pl.multiple_of(col * 16, 16), 16), :], ct)
    o_c = [local(co_v, cbar_out, osem.at[0])]

    r_fa.wait_recv()
    r_fb.wait_recv()
    across = group(2)
    r_core.append(send(across, across, rs.at[10], rr.at[10], dev(fc=1)))

    z_all = []
    for k in range(CH):
        x_dir[k].wait_recv()
        x_acc[k].wait_recv()
        v = ts[k, x] + xd[k] + xa[k]
        for q in range(NZ):
            zs[k, q] = v[4 * q : 4 * q + 4]
        z_all.append([
            send(zs.at[k, (zl + dz) % NZ], zr.at[k, dz - 1], zss.at[k, dz - 1], zrs.at[k, dz - 1], dev(dz=dz))
            for dz in range(1, NZ)
        ])

    for copy in r_core:
        copy.wait_recv()
    for p in range(8):
        v = jnp.concatenate([rg[4 * p + q] for q in range(4)], axis=0)
        high, low = split(v)
        rh_v[16 * p : 16 * (p + 1), :] = high
        rl_v[16 * p : 16 * (p + 1), :] = low

    cn = ctn.T
    ch, cl = split(cn)
    x3_v[...] = jnp.concatenate([ch, cl, ch], axis=1)
    bb_c.wait()
    for k in range(CH):
        where = slice(k * CW, (k + 1) * CW)
        r3 = jnp.concatenate([rh_v[:, where], rh_v[:, where], rl_v[:, where]], axis=0)
        bbar_v[:, where] = bbar_v[:, where] - dot(x3_v[...], r3, precision=None)
        o_c.append(
            local(bbar_v.at[:, pl.ds(k * CW, CW)], bbar_out.at[:, pl.ds(k * CW, CW)], osem.at[3 + k])
        )

    for copy in m_y:
        copy.wait_recv()
    d_c.wait()
    mt_full = mg[...].reshape(128, 128)
    product = dot(w_v[...], mt_full, ((1,), (1,)))
    mid = d_v[...] - jnp.where(rows >= cols, product, 0.0)
    z = dot(l_v[...].T, mid)
    q = jnp.where(rows >= cols, z, z.T)
    w8 = w_v[pl.ds(pl.multiple_of(row // 2 * 8, 8), 8), :]
    wq = dot(w8, q)
    a8 = dot(wq, w_v[...], ((1,), (1,)))
    a4 = jnp.where(core == 0, a8[:4], a8[4:])
    row4 = lax.broadcasted_iota(jnp.int32, (4, 128), 0) + row * 4
    col4 = lax.broadcasted_iota(jnp.int32, (4, 128), 1)
    kda = jnp.where(row4 > col4, a4, jnp.where(row4 == col4, 0.5 * a4, 0.0))
    pick = lax.broadcasted_iota(jnp.int32, (128, 16), 0) == (
        lax.broadcasted_iota(jnp.int32, (128, 16), 1) + col * 16
    )
    kd_v[...] = dot(kda, jnp.where(pick, 1.0, 0.0))
    o_c.append(local(kd_v, kda_out, osem.at[1]))

    ap = dot(wq, wp_v[...], ((1,), (1,)))
    ah, al = split(ap)
    a3 = jnp.concatenate([ah, al, ah], axis=1)
    for k in range(CH):
        where = slice(k * CW, (k + 1) * CW)
        r3 = jnp.concatenate([rh_v[:, where], rh_v[:, where], rl_v[:, where]], axis=0)
        corr = dot(a3, r3, precision=None)
        corr = jnp.where(core == 0, corr[:4], corr[4:])
        acc = zs[k, zl]
        for dz in range(1, NZ):
            z_all[k][dz - 1].wait_recv()
            acc = acc + zr[k, dz - 1]
        ro_v[:, where] = rbar_v_read(rb_c, rbar_v, k, where) - acc - corr
    o_c.append(local(ro_v, rbar_out, osem.at[2]))

    for copy in o_c:
        copy.wait()
    for copy in sent:
        copy.wait_send()


def rbar_v_read(copy, ref, k, where):
    if k == 0:
        copy.wait()
    return ref[:, where]


def body(c_panel, cbar_in, factor, dbar_in, r_panel, rbar_in, b_block, bbar_in):
    vmem = pltpu.VMEM
    sem = pltpu.SemaphoreType.DMA
    scratch = [
        vmem((128, 128), F32), vmem((128, 128), F32), vmem((16, 512), F32), vmem((4, 2048), F32),
        vmem((512, 2048), F32), vmem((512, 2048), F32), vmem((512, 2048), BF16), vmem((512, 2048), BF16),
        vmem((8, 16, 512), F32), vmem((32, 4, 2048), F32), vmem((128, 128), F32), vmem((128, 128), F32),
        vmem((512, 384), BF16), vmem((128, 2048), BF16), vmem((128, 2048), BF16),
        vmem((CH, 2, 64, CW), F32), vmem((CH, 64, CW), F32), vmem((CH, NX, 16, CW), F32),
        vmem((CH, 16, CW), F32), vmem((CH, 16, CW), F32), vmem((CH, 16, CW), F32), vmem((CH, 16, CW), F32),
        vmem((CH, NZ, 4, CW), F32), vmem((CH, NZ - 1, 4, CW), F32),
        vmem((16, 128), F32), vmem((7, 16, 128), F32), vmem((16, 128), F32), vmem((7, 16, 128), F32),
        vmem((8, 16, 128), F32),
        vmem((16, 512), F32), vmem((4, 16), F32), vmem((4, 2048), F32),
        sem((7,)), sem((CH,)), sem((3 + CH,)),
        sem((7,)), sem((7,)), sem((11,)), sem((11,)), sem((CH,)), sem((CH,)),
        sem((CH, 3)), sem((CH, 3)), sem((CH, 3)), sem((CH, 3)), sem((17,)), sem((17,)),
    ]
    cbar_t, bbar_out, kda, rbar_out = pl.pallas_call(
        kernel,
        out_shape=(
            jax.ShapeDtypeStruct((16, 512), F32),
            jax.ShapeDtypeStruct((512, 2048), F32),
            jax.ShapeDtypeStruct((4, 16), F32),
            jax.ShapeDtypeStruct((4, 2048), F32),
        ),
        in_specs=[pl.BlockSpec(memory_space=ANY)] * 8,
        out_specs=[pl.BlockSpec(memory_space=ANY)] * 4,
        scratch_shapes=scratch,
        compiler_params=pltpu.CompilerParams(
            collective_id=0, has_side_effects=True, vmem_limit_bytes=56 * 1024 * 1024
        ),
        name="block_step",
    )(c_panel.T, cbar_in.T, factor, dbar_in, r_panel, rbar_in, b_block, bbar_in)
    return cbar_t.T, bbar_out, kda, rbar_out


def solution(mesh):
    spec = P("row", "col")
    in_specs = (spec, spec, P(), P(), spec, spec, spec, spec)
    return jax.shard_map(
        body, mesh=mesh, in_specs=in_specs, out_specs=(spec,) * 4, check_vma=False
    )
```

time: 470 us -> 46.9 us (0.10)
  waiting for transfers between devices: 340 us -> 0 us
  blocking collectives: 80.6 us -> 0 us
  Pallas kernels: 0 us -> 38.8 us
  matrix products: 17.2 us -> 0 us
  between operations: 14.8 us -> 0.65 us
  other arithmetic: 10.8 us -> 0 us
    psum x1 -> x0, waiting for transfers between devices: 283 us -> none  [body(): product = lax.psum(product, 'row')]
    all_gather x2 -> x0, blocking collectives: 80.6 us -> none  [the longest x1 41.7 us: body(): lax.all_gather(c_panel, 'col', axis=1, tiled=True)]
    all_gather x1 -> x0, waiting for transfers between devices: 56.3 us -> none  [body(): r_full = lax.all_gather(r_panel, 'row', axis=0, tiled=True)]
    pallas_call x0 -> x1, Pallas kernels: none -> 38.8 us  [body(): pl.pallas_call(kernel, out_shape=(jax.ShapeDtypeStruct((16, 512), F32), j...]
    dot_general x5 -> x0, matrix products: 16.3 us -> none  [the longest x1 6.59 us: body(): jnp.dot(cbar_new, r_full, precision=highest, preferred_element_type=jnp.f...]
    another operation x2 -> x0, other arithmetic: 10.7 us -> none  [body(): jax.scipy.linalg.solve_triangular(factor_diagonal_block, column_adjoint_w...]
    unnamed x10 -> x8, local copies, waits for them, and re-layouts: 2.19 us -> 7.29 us
  transfers between devices with their start and end apart: 2 -> 0, of which waited for: 2 -> 0; matrix products, arithmetic and copies ran while one was open for 1% -> 0% of each run, Pallas kernels for 0% -> 0%
where the time goes in v1:
time: 46.9 us; the launch traced here: 46.8 us
  Pallas kernels  38.8 us (83%)
  local copies, waits for them, and re-layouts  7.29 us (16%)
  between operations  0.65 us (1%)
    pallas_call x1, Pallas kernels, body(): pl.pallas_call(kernel, out_shape=(jax.ShapeDtypeStruct((16, 512), F32), j...  38.8 us
    unnamed x8, local copies, waits for them, and re-layouts  7.29 us

profile of v1, /device:TPU:1, one launch (start us, length us, event | category | flops | bytes accessed | tf_op | source)
XLA Modules:
  0.0 46.8 jit_solution(9644754576083003598)
XLA Ops:
  0.6 38.8 %block_step.1 = (f32[16,512]{1,0:T(8,128)}, f32[512,2048]{1,0:T(8,128)}, f32[4,16]{1,0:T(4,128)}, f32[4,2048]{1,0:T(4,128)}) custom-call(f32[16,512]{1,0:T(8,128)} %bitcast.3, f32[16,512]{1,0:T(8,128)} %bitcast.4, f32[128,128]{1,0:T(8,128)} %l_hbm.1, f32[128,128]{1,0:T(8,128)} %d_hbm.1, f32[4,2048]{1,0:T(4,128)} %r_hbm.1, f32[4,2048]{1,0:T(4,128)} %rbar_hbm.1, ...), custom_call_target="tpu_custom_call" | custom-call | tf_op jit(solution)/shard_map/block_step/pallas_call | solution.py:346
  39.5 1.4 %copy.16 = f32[512,16]{0,1:T(8,128)} copy(f32[512,16]{0,1:T(8,128)} %bitcast.5) | data formatting | bytes 65536
  40.9 0.0 copy-start.1
  40.9 0.0 copy-start
  40.9 4.7 %copy.17 = f32[512,2048]{1,0:T(8,128)} copy(f32[512,2048]{1,0:T(8,128)} %get-tuple-element.17) | data formatting | bytes 8388608
  45.6 0.0 copy-done.1
  45.6 0.6 %copy.18 = f32[4,16]{1,0:T(4,128)} copy(f32[4,16]{1,0:T(4,128)S(1)} %copy-done.1) | data formatting | bytes 512
  46.2 0.0 copy-done
  46.2 0.6 %copy.19 = f32[4,2048]{1,0:T(4,128)} copy(f32[4,2048]{1,0:T(4,128)S(1)} %copy-done) | data formatting | bytes 65536
Async XLA Ops:
  40.9 4.7 %copy-start.1 = (f32[4,16]{1,0:T(4,128)S(1)}, f32[4,16]{1,0:T(4,128)}, u32[]{:S(2)}) copy-start(f32[4,16]{1,0:T(4,128)} %get-tuple-element.18) | copy-start | bytes 772
  40.9 5.3 %copy-start = (f32[4,2048]{1,0:T(4,128)S(1)}, f32[4,2048]{1,0:T(4,128)}, u32[]{:S(2)}) copy-start(f32[4,2048]{1,0:T(4,128)} %get-tuple-element.19) | copy-start | bytes 98308

commit v2 on v1

v2 whole, which is shorter than its diff:
```python
import jax
import jax.numpy as jnp
from jax import lax
from jax.experimental import pallas as pl
from jax.experimental.pallas import tpu as pltpu
from jax.sharding import PartitionSpec as P

F32 = jnp.float32
BF16 = jnp.bfloat16
HI = lax.Precision.HIGHEST
MESH = pl.DeviceIdType.MESH
NX, NZ, NY, NC, NH = 4, 4, 4, 2, 2
CH = 4
CW = 512


def dot(a, b, contract=((1,), (0,)), precision=HI):
    return lax.dot_general(
        a, b, (contract, ((), ())), precision=precision, preferred_element_type=F32
    )


def split(a):
    high = a.astype(BF16)
    return high, (a - high.astype(F32)).astype(BF16)


def kernel(
    c_hbm, cbar_hbm, l_hbm, d_hbm, r_hbm, rbar_hbm, b_hbm, bbar_hbm,
    cbar_out, bbar_out, kda_out, rbar_out,
    l_v, d_v, cc, rbar_v, b_v, bbar_v, bh_v, bl_v,
    cg, rg, w_v, wk_v, wp_v, x3_v, rh_v, rl_v,
    tb, tc, ts, xr, zs, zr,
    ms, ma, mt, mb, mg,
    lsem, bsem,
    cgs, cgr, rs, rr, tss, trs, xss, xrs, zss, zrs, mss, mrs,
):
    row, col = lax.axis_index("row"), lax.axis_index("col")
    core, x, zl = row % NC, (row // NC) % NX, row // (NC * NX)
    y, zh = col // NH, col % NH

    def dev(dz=0, dx=0, fc=0, dy=0, fz=0):
        c2 = 1 - core if fc else core
        h2 = 1 - zh if fz else zh
        z2, x2, y2 = (zl + dz) % NZ, (x + dx) % NX, (y + dy) % NY
        return (z2 * (NX * NC) + x2 * NC + c2, y2 * NH + h2)

    xc = [(dx, fc) for dx in range(NX) for fc in range(NC)][1:]
    zz = [(dz, fz) for dz in range(NZ) for fz in range(NH)][1:]
    peers = [dev(dz=dz, fz=fz) for dz, fz in reversed(zz)]
    peers += [dev(dy=dy) for dy in (2, 1, 3)]
    peers += [dev(dx=dx, fc=fc) for dx, fc in xc]

    barrier = pltpu.get_barrier_semaphore()
    for peer in peers:
        pl.semaphore_signal(barrier, inc=1, device_id=peer, device_id_type=MESH)

    pending = []

    def local(src, dst, sem):
        copy = pltpu.make_async_copy(src, dst, sem)
        copy.start()
        pending.append(copy)
        return copy

    def landed(copy):
        copy.wait()
        pending[:] = [other for other in pending if other is not copy]

    sent = []

    def send(src, dst, ssem, rsem, to):
        copy = pltpu.make_async_remote_copy(
            src_ref=src, dst_ref=dst, send_sem=ssem, recv_sem=rsem,
            device_id=to, device_id_type=MESH,
        )
        copy.start()
        sent.append(copy)
        return copy

    def end():
        for copy in pending:
            copy.wait()
        for copy in sent:
            copy.wait_send()

    my_slot = core * (NX * NZ) + x * NZ + zl
    l_c = local(l_hbm, l_v, lsem.at[0])
    cg_c = local(cbar_hbm, cg.at[zh, y], lsem.at[1])
    c_c = local(c_hbm, cc.at[zh], lsem.at[2])
    r_c = local(r_hbm, rg.at[my_slot], lsem.at[3])
    d_c = local(d_hbm, d_v, lsem.at[4])
    rb_c = local(rbar_hbm, rbar_v, lsem.at[5])
    b_c = [
        local(b_hbm.at[:, pl.ds(k * CW, CW)], b_v.at[:, pl.ds(k * CW, CW)], bsem.at[k])
        for k in range(CH)
    ]
    bb_c = local(bbar_hbm, bbar_v, lsem.at[6])

    pl.semaphore_wait(barrier, len(peers))

    cz = send(cbar_hbm, cg.at[zh, y], cgs.at[0], cgr.at[0], dev(fz=1))
    cc_z = send(c_hbm, cc.at[zh], cgs.at[7], cgr.at[7], dev(fz=1))
    cy = [
        send(cbar_hbm, cg.at[zh, y], cgs.at[dy], cgr.at[dy], dev(dy=dy)) for dy in (2, 1, 3)
    ]
    rz = [
        send(r_hbm, rg.at[my_slot], rs.at[dz - 1], rr.at[dz - 1], dev(dz=dz))
        for dz in range(1, NZ)
    ]

    rows = lax.broadcasted_iota(jnp.int32, (128, 128), 0)
    cols = lax.broadcasted_iota(jnp.int32, (128, 128), 1)
    landed(l_c)
    u = l_v[...].T
    eye = rows == cols
    w = jnp.where(eye, 1.0 / jnp.where(eye, u, 1.0), 0.0)
    for s in (1, 2, 4, 8, 16, 32, 64):
        mask = (rows // (2 * s) == cols // (2 * s)) & (rows % (2 * s) < s) & (cols % (2 * s) >= s)
        w = w - dot(dot(w, jnp.where(mask, u, 0.0)), w)
    w_v[...] = w

    cz.wait_recv()
    part = cg.at[1 - zh, y]
    cy2 = [send(part, part, cgs.at[3 + dy], cgr.at[3 + dy], dev(dy=dy)) for dy in (2, 1, 3)]

    for copy in cy:
        copy.wait_recv()
    cc_z.wait_recv()
    landed(cg_c)
    landed(c_c)
    pt = dot(cc[...].reshape(32, 512), cg[zh].reshape(64, 512), ((1,), (1,)))
    ms[...] = jnp.concatenate([pt[:16], pt[16:]], axis=1)
    m_x = [
        send(ms, ma.at[i], mss.at[i], mrs.at[i], dev(dx=dx, fc=fc))
        for i, (dx, fc) in enumerate(xc)
    ]

    for copy in rz:
        copy.wait_recv()
    landed(r_c)

    def group(g):
        return rg.at[pl.ds(core * (NX * NZ) + ((x + g) % NX) * NZ, NZ)]

    own = group(0)
    r_x = [send(own, own, rs.at[2 + dx], rr.at[2 + dx], dev(dx=dx)) for dx in (2, 1, 3)]
    r_core = [send(own, own, rs.at[6], rr.at[6], dev(fc=1))]

    natural = ((cols % 64) // 16 * 2 + cols // 64) * 16 + cols % 16
    wk = dot(w, jnp.where(rows == natural, 1.0, 0.0))
    wk_v[...] = wk
    natural = (rows % 16) // 4 * 32 + (rows // 16) % 4 * 8 + rows // 64 * 4 + rows % 4
    order = jnp.where(cols == natural, 1.0, 0.0)
    wp_v[...] = dot(order, w)
    wpk = dot(order, wk)

    for k in range(CH):
        landed(b_c[k])
        high, low = split(b_v[:, k * CW : (k + 1) * CW])
        bh_v[:, k * CW : (k + 1) * CW] = high
        bl_v[:, k * CW : (k + 1) * CW] = low

    for copy in cy2:
        copy.wait_recv()
    ct = cg[...].reshape(128, 512)
    ctn = dot(wpk, ct)
    nh, nl = split(ctn)
    both = jnp.concatenate([nh, nl], axis=0)

    def chunk(k):
        where = slice(k * CW, (k + 1) * CW)
        p = dot(both, bh_v[:, where], precision=None)
        t = p[:128] + p[128:] + dot(nh, bl_v[:, where], precision=None)
        tb[k, 0] = t[:64]
        tb[k, 1] = t[64:]
        return send(tb.at[k, 1 - core], tc.at[k], tss.at[k], trs.at[k], dev(fc=1))

    def after_core(k):
        t_core[k].wait_recv()
        v = tb[k, core] + tc[k]
        for q in range(NX):
            ts[k, q] = v[16 * q : 16 * (q + 1)]
        return [
            send(ts.at[k, (x + dx) % NX], xr.at[k, dx - 1], xss.at[k, dx - 1], xrs.at[k, dx - 1], dev(dx=dx))
            for dx in (2, 1, 3)
        ]

    t_core, t_x = [chunk(0)], []

    total = ms[...]
    for i, copy in enumerate(m_x):
        copy.wait_recv()
        total = total + ma[i]
    mt[...] = total
    m_z = [
        send(mt, mb.at[i], mss.at[7 + i], mrs.at[7 + i], dev(dz=dz, fz=fz))
        for i, (dz, fz) in enumerate(zz)
    ]

    t_core.append(chunk(1))
    t_x.append(after_core(0))
    t_core.append(chunk(2))
    t_x.append(after_core(1))
    t_core.append(chunk(3))
    t_x.append(after_core(2))
    t_x.append(after_core(3))

    for i, copy in enumerate(r_x):
        copy.wait_recv()
    for dx in range(1, NX):
        r_core.append(send(group(dx), group(dx), rs.at[6 + dx], rr.at[6 + dx], dev(fc=1)))

    cbar_out[...] = dot(wk_v[pl.ds(pl.multiple_of(col * 16, 16), 16), :], ct)
    cn = ctn.T
    ch, cl = split(cn)
    x3_v[...] = jnp.concatenate([ch, cl, ch], axis=1)

    same, other = mt[...], None
    for i, (dz, fz) in enumerate(zz):
        m_z[i].wait_recv()
        if fz:
            other = mb[i] if other is None else other + mb[i]
        else:
            same = same + mb[i]
    mg[y, zh] = same
    mg[y, 1 - zh] = other
    m_y = [
        send(mg.at[y], mg.at[y], mss.at[13 + dy], mrs.at[13 + dy], dev(dy=dy)) for dy in (2, 1, 3)
    ]

    for copy in r_core:
        copy.wait_recv()
    for p in range(8):
        v = jnp.concatenate([rg[4 * p + q] for q in range(4)], axis=0)
        high, low = split(v)
        rh_v[16 * p : 16 * (p + 1), :] = high
        rl_v[16 * p : 16 * (p + 1), :] = low

    def r3(k):
        where = slice(k * CW, (k + 1) * CW)
        return jnp.concatenate([rh_v[:, where], rh_v[:, where], rl_v[:, where]], axis=0)

    landed(bb_c)
    for k in range(CH):
        where = slice(k * CW, (k + 1) * CW)
        bbar_out[:, where] = bbar_v[:, where] - dot(x3_v[...], r3(k), precision=None)

    def over_z(k):
        for copy in t_x[k]:
            copy.wait_recv()
        v = ts[k, x] + xr[k, 0] + xr[k, 1] + xr[k, 2]
        for q in range(NZ):
            zs[k, q] = v[4 * q : 4 * q + 4]
        return [
            send(zs.at[k, (zl + dz) % NZ], zr.at[k, dz - 1], zss.at[k, dz - 1], zrs.at[k, dz - 1], dev(dz=dz))
            for dz in range(1, NZ)
        ]

    t_z = [over_z(0), over_z(1)]

    for copy in m_y:
        copy.wait_recv()
    landed(d_c)
    parts = []
    for q in range(NY):
        for h in range(NH):
            lanes = slice(64 * h, 64 * h + 64)
            parts.append(jnp.concatenate([mg[q, 0][:, lanes], mg[q, 1][:, lanes]], axis=1))
    mt_full = jnp.concatenate(parts, axis=0)
    product = dot(wk_v[...], mt_full, ((1,), (1,)))
    mid = d_v[...] - jnp.where(rows >= cols, product, 0.0)
    z = dot(l_v[...].T, mid)
    q = jnp.where(rows >= cols, z, z.T)
    w8 = w_v[pl.ds(pl.multiple_of(row // 2 * 8, 8), 8), :]
    wq = dot(w8, q)
    a8 = dot(wq, w_v[...], ((1,), (1,)))
    a4 = jnp.where(core == 0, a8[:4], a8[4:])
    row4 = lax.broadcasted_iota(jnp.int32, (4, 128), 0) + row * 4
    col4 = lax.broadcasted_iota(jnp.int32, (4, 128), 1)
    kda = jnp.where(row4 > col4, a4, jnp.where(row4 == col4, 0.5 * a4, 0.0))
    pick = lax.broadcasted_iota(jnp.int32, (128, 16), 0) == (
        lax.broadcasted_iota(jnp.int32, (128, 16), 1) + col * 16
    )
    kda_out[...] = dot(kda, jnp.where(pick, 1.0, 0.0))

    ap = dot(wq, wp_v[...], ((1,), (1,)))
    ah, al = split(ap)
    a3 = jnp.concatenate([ah, al, ah], axis=1)
    landed(rb_c)
    for k in range(CH):
        where = slice(k * CW, (k + 1) * CW)
        corr = dot(a3, r3(k), precision=None)
        rbar_v[:, where] = rbar_v[:, where] - jnp.where(core == 0, corr[:4], corr[4:])

    t_z += [over_z(2), over_z(3)]
    for k in range(CH):
        where = slice(k * CW, (k + 1) * CW)
        acc = zs[k, zl]
        for dz in range(1, NZ):
            t_z[k][dz - 1].wait_recv()
            acc = acc + zr[k, dz - 1]
        rbar_out[:, where] = rbar_v[:, where] - acc
    end()


def store(cbar_v, bbar_v, kda_v, rbar_v, cbar_hbm, bbar_hbm, kda_hbm, rbar_hbm, sem):
    copies = [
        pltpu.make_async_copy(bbar_v.at[pl.ds(64 * k, 64)], bbar_hbm.at[pl.ds(64 * k, 64)], sem.at[3 + k])
        for k in range(8)
    ]
    copies += [
        pltpu.make_async_copy(cbar_v, cbar_hbm, sem.at[0]),
        pltpu.make_async_copy(kda_v, kda_hbm, sem.at[1]),
        pltpu.make_async_copy(rbar_v, rbar_hbm, sem.at[2]),
    ]
    for copy in copies:
        copy.start()
    for copy in copies:
        copy.wait()


SHAPES = ((16, 512), (512, 2048), (4, 16), (4, 2048))


def body(c_panel, cbar_in, factor, dbar_in, r_panel, rbar_in, b_block, bbar_in):
    vmem = pltpu.VMEM
    sem = pltpu.SemaphoreType.DMA
    anywhere = pl.BlockSpec(memory_space=pl.ANY)
    in_vmem = pl.BlockSpec(memory_space=vmem)
    scratch = [
        vmem((128, 128), F32), vmem((128, 128), F32), vmem((2, 16, 512), F32), vmem((4, 2048), F32),
        vmem((512, 2048), F32), vmem((512, 2048), F32), vmem((512, 2048), BF16), vmem((512, 2048), BF16),
        vmem((NH, NY, 16, 512), F32), vmem((32, 4, 2048), F32),
        vmem((128, 128), F32), vmem((128, 128), F32), vmem((128, 128), F32),
        vmem((512, 384), BF16), vmem((128, 2048), BF16), vmem((128, 2048), BF16),
        vmem((CH, 2, 64, CW), F32), vmem((CH, 64, CW), F32), vmem((CH, NX, 16, CW), F32),
        vmem((CH, NX - 1, 16, CW), F32),
        vmem((CH, NZ, 4, CW), F32), vmem((CH, NZ - 1, 4, CW), F32),
        vmem((16, 128), F32), vmem((7, 16, 128), F32), vmem((16, 128), F32), vmem((7, 16, 128), F32),
        vmem((NY, NH, 16, 128), F32),
        sem((7,)), sem((CH,)),
        sem((8,)), sem((8,)), sem((10,)), sem((10,)), sem((CH,)), sem((CH,)),
        sem((CH, 3)), sem((CH, 3)), sem((CH, 3)), sem((CH, 3)), sem((17,)), sem((17,)),
    ]
    args = (c_panel.T, cbar_in.T, factor, dbar_in, r_panel, rbar_in, b_block, bbar_in)
    args = [pltpu.with_memory_space_constraint(a, pltpu.HBM) for a in args]
    results = pl.pallas_call(
        kernel,
        out_shape=[vmem(shape, F32) for shape in SHAPES],
        in_specs=[anywhere] * 8,
        out_specs=[in_vmem] * 4,
        scratch_shapes=scratch,
        compiler_params=pltpu.CompilerParams(
            collective_id=0, has_side_effects=True, vmem_limit_bytes=32 * 1024 * 1024
        ),
        name="block_step",
    )(*args)
    results = [pltpu.with_memory_space_constraint(a, vmem) for a in results]
    cbar_t, bbar_out, kda, rbar_out = pl.pallas_call(
        store,
        out_shape=[jax.ShapeDtypeStruct(shape, F32) for shape in SHAPES],
        in_specs=[anywhere] * 4,
        out_specs=[anywhere] * 4,
        scratch_shapes=[sem((11,))],
        compiler_params=pltpu.CompilerParams(vmem_limit_bytes=4 * 1024 * 1024),
        name="store",
    )(*results)
    return cbar_t.T, bbar_out, kda, rbar_out


def solution(mesh):
    spec = P("row", "col")
    in_specs = (spec, spec, P(), P(), spec, spec, spec, spec)
    return jax.shard_map(
        body, mesh=mesh, in_specs=in_specs, out_specs=(spec,) * 4, check_vma=False
    )
```

time: 46.9 us -> 39 us (0.83)
  local copies, waits for them, and re-layouts: 7.29 us -> 0 us
  Pallas kernels: 38.8 us -> 38 us
    unnamed x8 -> x0, local copies, waits for them, and re-layouts: 7.29 us -> none
    pallas_call x1 -> x2, Pallas kernels: 38.8 us -> 38 us  [the longest x1 35.9 us: body(): pl.pallas_call(kernel, out_shape=[vmem(shape, F32) for shape in SHAPES],...]
where the time goes in v2:
time: 39 us; the launch traced here: 38.7 us
  Pallas kernels  38 us (97%)
  between operations  0.64 us (2%)
    pallas_call x1, Pallas kernels, body(): pl.pallas_call(kernel, out_shape=[vmem(shape, F32) for shape in SHAPES],...  35.9 us
    pallas_call x1, Pallas kernels, body(): pl.pallas_call(store, out_shape=[jax.ShapeDtypeStruct(shape, F32) for sha...  2.11 us

profile of v2, /device:TPU:1, one launch (start us, length us, event | category | flops | bytes accessed | tf_op | source)
XLA Modules:
  0.0 38.7 jit_solution(3156272986292023209)
XLA Ops:
  0.6 35.9 %block_step.1 = (f32[16,512]{1,0:T(8,128)S(1)}, f32[512,2048]{1,0:T(8,128)S(1)}, f32[4,16]{1,0:T(4,128)S(1)}, f32[4,2048]{1,0:T(4,128)S(1)}) custom-call(f32[16,512]{1,0:T(8,128)} %bitcast.3, f32[16,512]{1,0:T(8,128)} %bitcast.4, f32[128,128]{1,0:T(8,128)} %l_hbm.1, f32[128,128]{1,0:T(8,128)} %d_hbm.1, f32[4,2048]{1,0:T(4,128)} %r_hbm.1, ...), custom_call_target="tpu_custom_call" | custom-call | tf_op jit(solution)/shard_map/block_step/pallas_call | solution.py:348
  36.6 2.1 %store.1 = (f32[16,512]{1,0:T(8,128)}, f32[512,2048]{1,0:T(8,128)}, f32[4,16]{1,0:T(4,128)}, f32[4,2048]{1,0:T(4,128)}) custom-call(f32[16,512]{1,0:T(8,128)S(1)} %get-tuple-element.12.cbar_v, f32[512,2048]{1,0:T(8,128)S(1)} %get-tuple-element.13.bbar_v, f32[4,16]{1,0:T(4,128)S(1)} %get-tuple-element.14.kda_v, f32[4,2048]{1,0:T(4,128)S(1)} %get-tuple-element.15.rbar_v), custom_call_target="tpu_custom_call" | custom-call | tf_op jit(solution)/shard_map/store/pallas_call | solution.py:360

commit v3 on v2

--- a/solution.py
+++ b/solution.py
@@ -12,6 +12,7 @@
 NX, NZ, NY, NC, NH = 4, 4, 4, 2, 2
 CH = 4
 CW = 512
+ZK = 3
 
 
 def dot(a, b, contract=((1,), (0,)), precision=HI):
@@ -29,8 +30,8 @@
     c_hbm, cbar_hbm, l_hbm, d_hbm, r_hbm, rbar_hbm, b_hbm, bbar_hbm,
     cbar_out, bbar_out, kda_out, rbar_out,
     l_v, d_v, cc, rbar_v, b_v, bbar_v, bh_v, bl_v,
-    cg, rg, w_v, wk_v, wp_v, x3_v, rh_v, rl_v,
-    tb, tc, ts, xr, zs, zr,
+    cg, rg, w_v, wk_v, wpk_v, uk_v, dk_v, x3_v, rh_v, rl_v,
+    tb, tc, ts, xr, zs, zr, z1, zr1, x1, xr1,
     ms, ma, mt, mb, mg,
     lsem, bsem,
     cgs, cgr, rs, rr, tss, trs, xss, xrs, zss, zrs, mss, mrs,
@@ -87,7 +88,7 @@
     my_slot = core * (NX * NZ) + x * NZ + zl
     l_c = local(l_hbm, l_v, lsem.at[0])
     cg_c = local(cbar_hbm, cg.at[zh, y], lsem.at[1])
-    c_c = local(c_hbm, cc.at[zh], lsem.at[2])
+    c_c = local(c_hbm, cc.at[y], lsem.at[2])
     r_c = local(r_hbm, rg.at[my_slot], lsem.at[3])
     d_c = local(d_hbm, d_v, lsem.at[4])
     rb_c = local(rbar_hbm, rbar_v, lsem.at[5])
@@ -100,13 +101,16 @@
     pl.semaphore_wait(barrier, len(peers))
 
     cz = send(cbar_hbm, cg.at[zh, y], cgs.at[0], cgr.at[0], dev(fz=1))
-    cc_z = send(c_hbm, cc.at[zh], cgs.at[7], cgr.at[7], dev(fz=1))
     cy = [
         send(cbar_hbm, cg.at[zh, y], cgs.at[dy], cgr.at[dy], dev(dy=dy)) for dy in (2, 1, 3)
     ]
+    cc_y = [send(c_hbm, cc.at[y], cgs.at[6 + dy], cgr.at[6 + dy], dev(dy=dy)) for dy in (2, 1, 3)]
     rz = [
         send(r_hbm, rg.at[my_slot], rs.at[dz - 1], rr.at[dz - 1], dev(dz=dz))
         for dz in range(1, NZ)
+    ]
+    r_x = [
+        send(r_hbm, rg.at[my_slot], rs.at[2 + dx], rr.at[2 + dx], dev(dx=dx)) for dx in (2, 1, 3)
     ]
 
     rows = lax.broadcasted_iota(jnp.int32, (128, 128), 0)
@@ -119,41 +123,17 @@
         mask = (rows // (2 * s) == cols // (2 * s)) & (rows % (2 * s) < s) & (cols % (2 * s) >= s)
         w = w - dot(dot(w, jnp.where(mask, u, 0.0)), w)
     w_v[...] = w
-
-    cz.wait_recv()
-    part = cg.at[1 - zh, y]
-    cy2 = [send(part, part, cgs.at[3 + dy], cgr.at[3 + dy], dev(dy=dy)) for dy in (2, 1, 3)]
-
-    for copy in cy:
-        copy.wait_recv()
-    cc_z.wait_recv()
-    landed(cg_c)
-    landed(c_c)
-    pt = dot(cc[...].reshape(32, 512), cg[zh].reshape(64, 512), ((1,), (1,)))
-    ms[...] = jnp.concatenate([pt[:16], pt[16:]], axis=1)
-    m_x = [
-        send(ms, ma.at[i], mss.at[i], mrs.at[i], dev(dx=dx, fc=fc))
-        for i, (dx, fc) in enumerate(xc)
-    ]
-
-    for copy in rz:
-        copy.wait_recv()
-    landed(r_c)
-
-    def group(g):
-        return rg.at[pl.ds(core * (NX * NZ) + ((x + g) % NX) * NZ, NZ)]
-
-    own = group(0)
-    r_x = [send(own, own, rs.at[2 + dx], rr.at[2 + dx], dev(dx=dx)) for dx in (2, 1, 3)]
-    r_core = [send(own, own, rs.at[6], rr.at[6], dev(fc=1))]
-
-    natural = ((cols % 64) // 16 * 2 + cols // 64) * 16 + cols % 16
-    wk = dot(w, jnp.where(rows == natural, 1.0, 0.0))
+    order_c = ((cols % 64) // 16 * 2 + cols // 64) * 16 + cols % 16
+    wk = dot(w, jnp.where(rows == order_c, 1.0, 0.0))
     wk_v[...] = wk
+    order_r = ((rows % 64) // 16 * 2 + rows // 64) * 16 + rows % 16
+    uk_v[...] = dot(jnp.where(cols == order_r, 1.0, 0.0), u)
+    landed(d_c)
+    dk_v[...] = dot(d_v[...], jnp.where(rows == order_c, 1.0, 0.0))
     natural = (rows % 16) // 4 * 32 + (rows // 16) % 4 * 8 + rows // 64 * 4 + rows % 4
     order = jnp.where(cols == natural, 1.0, 0.0)
-    wp_v[...] = dot(order, w)
     wpk = dot(order, wk)
+    wpk_v[...] = wpk
 
     for k in range(CH):
         landed(b_c[k])
@@ -161,7 +141,37 @@
         bh_v[:, k * CW : (k + 1) * CW] = high
         bl_v[:, k * CW : (k + 1) * CW] = low
 
-    for copy in cy2:
+    cz.wait_recv()
+    part = cg.at[1 - zh, y]
+    cy2 = [send(part, part, cgs.at[3 + dy], cgr.at[3 + dy], dev(dy=dy)) for dy in (2, 1, 3)]
+
+    for copy in cc_y:
+        copy.wait_recv()
+    landed(cg_c)
+    landed(c_c)
+    pt = dot(jnp.concatenate([cg[0, y], cg[1, y]], axis=0), cc[...].reshape(64, 512), ((1,), (1,)))
+    ms[...] = jnp.concatenate([pt[:16], pt[16:]], axis=1)
+    m_x = [
+        send(ms, ma.at[i], mss.at[i], mrs.at[i], dev(dx=dx, fc=fc))
+        for i, (dx, fc) in enumerate(xc)
+    ]
+
+    for copy in rz:
+        copy.wait_recv()
+    landed(r_c)
+
+    def group(g):
+        return rg.at[pl.ds(core * (NX * NZ) + ((x + g) % NX) * NZ, NZ)]
+
+    for dz in range(1, NZ):
+        slot = rg.at[core * (NX * NZ) + x * NZ + (zl + dz) % NZ]
+        r_x += [
+            send(slot, slot, rs.at[3 * dz + 2 + dx], rr.at[3 * dz + 2 + dx], dev(dx=dx))
+            for dx in (2, 1, 3)
+        ]
+    r_core = [send(group(0), group(0), rs.at[15], rr.at[15], dev(fc=1))]
+
+    for copy in cy + cy2:
         copy.wait_recv()
     ct = cg[...].reshape(128, 512)
     ctn = dot(wpk, ct)
@@ -179,6 +189,14 @@
     def after_core(k):
         t_core[k].wait_recv()
         v = tb[k, core] + tc[k]
+        if k == ZK:
+            for q in range(NX):
+                for p in range(NZ):
+                    z1[p, q] = v[16 * q + 4 * p : 16 * q + 4 * p + 4]
+            return [
+                send(z1.at[(zl + dz) % NZ], zr1.at[dz - 1], zss.at[k, dz - 1], zrs.at[k, dz - 1], dev(dz=dz))
+                for dz in range(1, NZ)
+            ]
         for q in range(NX):
             ts[k, q] = v[16 * q : 16 * (q + 1)]
         return [
@@ -186,7 +204,8 @@
             for dx in (2, 1, 3)
         ]
 
-    t_core, t_x = [chunk(0)], []
+    t_core = [chunk(k) for k in range(CH)]
+    t_1 = [after_core(0)]
 
     total = ms[...]
     for i, copy in enumerate(m_x):
@@ -197,19 +216,12 @@
         send(mt, mb.at[i], mss.at[7 + i], mrs.at[7 + i], dev(dz=dz, fz=fz))
         for i, (dz, fz) in enumerate(zz)
     ]
-
-    t_core.append(chunk(1))
-    t_x.append(after_core(0))
-    t_core.append(chunk(2))
-    t_x.append(after_core(1))
-    t_core.append(chunk(3))
-    t_x.append(after_core(2))
-    t_x.append(after_core(3))
-
-    for i, copy in enumerate(r_x):
+    t_1 += [after_core(k) for k in range(1, CH)]
+
+    for copy in r_x:
         copy.wait_recv()
     for dx in range(1, NX):
-        r_core.append(send(group(dx), group(dx), rs.at[6 + dx], rr.at[6 + dx], dev(fc=1)))
+        r_core.append(send(group(dx), group(dx), rs.at[15 + dx], rr.at[15 + dx], dev(fc=1)))
 
     cbar_out[...] = dot(wk_v[pl.ds(pl.multiple_of(col * 16, 16), 16), :], ct)
     cn = ctn.T
@@ -246,9 +258,15 @@
         where = slice(k * CW, (k + 1) * CW)
         bbar_out[:, where] = bbar_v[:, where] - dot(x3_v[...], r3(k), precision=None)
 
-    def over_z(k):
-        for copy in t_x[k]:
+    def second_axis(k):
+        for copy in t_1[k]:
             copy.wait_recv()
+        if k == ZK:
+            x1[...] = z1[zl] + zr1[0] + zr1[1] + zr1[2]
+            return [
+                send(x1.at[(x + dx) % NX], xr1.at[dx - 1], xss.at[k, dx - 1], xrs.at[k, dx - 1], dev(dx=dx))
+                for dx in (2, 1, 3)
+            ]
         v = ts[k, x] + xr[k, 0] + xr[k, 1] + xr[k, 2]
         for q in range(NZ):
             zs[k, q] = v[4 * q : 4 * q + 4]
@@ -257,24 +275,22 @@
             for dz in range(1, NZ)
         ]
 
-    t_z = [over_z(0), over_z(1)]
+    t_2 = {k: second_axis(k) for k in (0, 1, ZK, 2)}
 
     for copy in m_y:
         copy.wait_recv()
-    landed(d_c)
     parts = []
     for q in range(NY):
         for h in range(NH):
             lanes = slice(64 * h, 64 * h + 64)
             parts.append(jnp.concatenate([mg[q, 0][:, lanes], mg[q, 1][:, lanes]], axis=1))
     mt_full = jnp.concatenate(parts, axis=0)
-    product = dot(wk_v[...], mt_full, ((1,), (1,)))
-    mid = d_v[...] - jnp.where(rows >= cols, product, 0.0)
-    z = dot(l_v[...].T, mid)
-    q = jnp.where(rows >= cols, z, z.T)
-    w8 = w_v[pl.ds(pl.multiple_of(row // 2 * 8, 8), 8), :]
+    mid = dk_v[...] - jnp.where(rows >= order_c, dot(w_v[...], mt_full), 0.0)
+    z = dot(uk_v[...], mid)
+    q = jnp.where(order_r >= order_c, z, z.T)
+    w8 = wk_v[pl.ds(pl.multiple_of(row // 2 * 8, 8), 8), :]
     wq = dot(w8, q)
-    a8 = dot(wq, w_v[...], ((1,), (1,)))
+    a8 = dot(wq, wk_v[...], ((1,), (1,)))
     a4 = jnp.where(core == 0, a8[:4], a8[4:])
     row4 = lax.broadcasted_iota(jnp.int32, (4, 128), 0) + row * 4
     col4 = lax.broadcasted_iota(jnp.int32, (4, 128), 1)
@@ -284,7 +300,7 @@
     )
     kda_out[...] = dot(kda, jnp.where(pick, 1.0, 0.0))
 
-    ap = dot(wq, wp_v[...], ((1,), (1,)))
+    ap = dot(wq, wpk_v[...], ((1,), (1,)))
     ah, al = split(ap)
     a3 = jnp.concatenate([ah, al, ah], axis=1)
     landed(rb_c)
@@ -292,14 +308,14 @@
         where = slice(k * CW, (k + 1) * CW)
         corr = dot(a3, r3(k), precision=None)
         rbar_v[:, where] = rbar_v[:, where] - jnp.where(core == 0, corr[:4], corr[4:])
-
-    t_z += [over_z(2), over_z(3)]
     for k in range(CH):
         where = slice(k * CW, (k + 1) * CW)
-        acc = zs[k, zl]
-        for dz in range(1, NZ):
-            t_z[k][dz - 1].wait_recv()
-            acc = acc + zr[k, dz - 1]
+        for copy in t_2[k]:
+            copy.wait_recv()
+        if k == ZK:
+            acc = x1[x] + xr1[0] + xr1[1] + xr1[2]
+        else:
+            acc = zs[k, zl] + zr[k, 0] + zr[k, 1] + zr[k, 2]
         rbar_out[:, where] = rbar_v[:, where] - acc
     end()
 
@@ -329,18 +345,21 @@
     anywhere = pl.BlockSpec(memory_space=pl.ANY)
     in_vmem = pl.BlockSpec(memory_space=vmem)
     scratch = [
-        vmem((128, 128), F32), vmem((128, 128), F32), vmem((2, 16, 512), F32), vmem((4, 2048), F32),
+        vmem((128, 128), F32), vmem((128, 128), F32), vmem((NY, 16, 512), F32), vmem((4, 2048), F32),
         vmem((512, 2048), F32), vmem((512, 2048), F32), vmem((512, 2048), BF16), vmem((512, 2048), BF16),
         vmem((NH, NY, 16, 512), F32), vmem((32, 4, 2048), F32),
         vmem((128, 128), F32), vmem((128, 128), F32), vmem((128, 128), F32),
+        vmem((128, 128), F32), vmem((128, 128), F32),
         vmem((512, 384), BF16), vmem((128, 2048), BF16), vmem((128, 2048), BF16),
         vmem((CH, 2, 64, CW), F32), vmem((CH, 64, CW), F32), vmem((CH, NX, 16, CW), F32),
         vmem((CH, NX - 1, 16, CW), F32),
         vmem((CH, NZ, 4, CW), F32), vmem((CH, NZ - 1, 4, CW), F32),
+        vmem((NZ, NX, 4, CW), F32), vmem((NZ - 1, NX, 4, CW), F32),
+        vmem((NX, 4, CW), F32), vmem((NX - 1, 4, CW), F32),
         vmem((16, 128), F32), vmem((7, 16, 128), F32), vmem((16, 128), F32), vmem((7, 16, 128), F32),
         vmem((NY, NH, 16, 128), F32),
         sem((7,)), sem((CH,)),
-        sem((8,)), sem((8,)), sem((10,)), sem((10,)), sem((CH,)), sem((CH,)),
+        sem((10,)), sem((10,)), sem((19,)), sem((19,)), sem((CH,)), sem((CH,)),
         sem((CH, 3)), sem((CH, 3)), sem((CH, 3)), sem((CH, 3)), sem((17,)), sem((17,)),
     ]
     args = (c_panel.T, cbar_in.T, factor, dbar_in, r_panel, rbar_in, b_block, bbar_in)

time: 39 us -> 35.9 us (0.921)
  Pallas kernels: 38 us -> 35.2 us
    pallas_call x1, Pallas kernels: 35.9 us -> 33.1 us  [body(): pl.pallas_call(kernel, out_shape=[vmem(shape, F32) for shape in SHAPES],...]
where the time goes in v3:
time: 35.9 us; the launch traced here: 35.8 us
  Pallas kernels  35.2 us (98%)
  between operations  0.64 us (2%)
    pallas_call x1, Pallas kernels, body(): pl.pallas_call(kernel, out_shape=[vmem(shape, F32) for shape in SHAPES],...  33.1 us
    pallas_call x1, Pallas kernels, body(): pl.pallas_call(store, out_shape=[jax.ShapeDtypeStruct(shape, F32) for sha...  2.11 us

profile of v3, /device:TPU:1, one launch (start us, length us, event | category | flops | bytes accessed | tf_op | source)
XLA Modules:
  0.0 35.8 jit_solution(15875267130558000430)
XLA Ops:
  0.6 33.1 %block_step.1 = (f32[16,512]{1,0:T(8,128)S(1)}, f32[512,2048]{1,0:T(8,128)S(1)}, f32[4,16]{1,0:T(4,128)S(1)}, f32[4,2048]{1,0:T(4,128)S(1)}) custom-call(f32[16,512]{1,0:T(8,128)} %bitcast.3, f32[16,512]{1,0:T(8,128)} %bitcast.4, f32[128,128]{1,0:T(8,128)} %l_hbm.1, f32[128,128]{1,0:T(8,128)} %d_hbm.1, f32[4,2048]{1,0:T(4,128)} %r_hbm.1, ...), custom_call_target="tpu_custom_call" | custom-call | tf_op jit(solution)/shard_map/block_step/pallas_call | solution.py:367
  33.7 2.1 %store.1 = (f32[16,512]{1,0:T(8,128)}, f32[512,2048]{1,0:T(8,128)}, f32[4,16]{1,0:T(4,128)}, f32[4,2048]{1,0:T(4,128)}) custom-call(f32[16,512]{1,0:T(8,128)S(1)} %get-tuple-element.12.cbar_v, f32[512,2048]{1,0:T(8,128)S(1)} %get-tuple-element.13.bbar_v, f32[4,16]{1,0:T(4,128)S(1)} %get-tuple-element.14.kda_v, f32[4,2048]{1,0:T(4,128)S(1)} %get-tuple-element.15.rbar_v), custom_call_target="tpu_custom_call" | custom-call | tf_op jit(solution)/shard_map/store/pallas_call | solution.py:379

commit v4 on v3

--- a/solution.py
+++ b/solution.py
@@ -123,6 +123,37 @@
         mask = (rows // (2 * s) == cols // (2 * s)) & (rows % (2 * s) < s) & (cols % (2 * s) >= s)
         w = w - dot(dot(w, jnp.where(mask, u, 0.0)), w)
     w_v[...] = w
+
+
+    cz.wait_recv()
+    part = cg.at[1 - zh, y]
+    cy2 = [send(part, part, cgs.at[3 + dy], cgr.at[3 + dy], dev(dy=dy)) for dy in (2, 1, 3)]
+
+    for copy in cc_y:
+        copy.wait_recv()
+    landed(cg_c)
+    landed(c_c)
+    pt = dot(jnp.concatenate([cg[0, y], cg[1, y]], axis=0), cc[...].reshape(64, 512), ((1,), (1,)))
+    ms[...] = jnp.concatenate([pt[:16], pt[16:]], axis=1)
+    m_x = [
+        send(ms, ma.at[i], mss.at[i], mrs.at[i], dev(dx=dx, fc=fc))
+        for i, (dx, fc) in enumerate(xc)
+    ]
+
+    for copy in rz:
+        copy.wait_recv()
+    landed(r_c)
+
+    def group(g):
+        return rg.at[pl.ds(core * (NX * NZ) + ((x + g) % NX) * NZ, NZ)]
+
+    for dz in range(1, NZ):
+        slot = rg.at[core * (NX * NZ) + x * NZ + (zl + dz) % NZ]
+        r_x += [
+            send(slot, slot, rs.at[3 * dz + 2 + dx], rr.at[3 * dz + 2 + dx], dev(dx=dx))
+            for dx in (2, 1, 3)
+        ]
+    r_core = [send(group(0), group(0), rs.at[15], rr.at[15], dev(fc=1))]
     order_c = ((cols % 64) // 16 * 2 + cols // 64) * 16 + cols % 16
     wk = dot(w, jnp.where(rows == order_c, 1.0, 0.0))
     wk_v[...] = wk
@@ -140,36 +171,6 @@
         high, low = split(b_v[:, k * CW : (k + 1) * CW])
         bh_v[:, k * CW : (k + 1) * CW] = high
         bl_v[:, k * CW : (k + 1) * CW] = low
-
-    cz.wait_recv()
-    part = cg.at[1 - zh, y]
-    cy2 = [send(part, part, cgs.at[3 + dy], cgr.at[3 + dy], dev(dy=dy)) for dy in (2, 1, 3)]
-
-    for copy in cc_y:
-        copy.wait_recv()
-    landed(cg_c)
-    landed(c_c)
-    pt = dot(jnp.concatenate([cg[0, y], cg[1, y]], axis=0), cc[...].reshape(64, 512), ((1,), (1,)))
-    ms[...] = jnp.concatenate([pt[:16], pt[16:]], axis=1)
-    m_x = [
-        send(ms, ma.at[i], mss.at[i], mrs.at[i], dev(dx=dx, fc=fc))
-        for i, (dx, fc) in enumerate(xc)
-    ]
-
-    for copy in rz:
-        copy.wait_recv()
-    landed(r_c)
-
-    def group(g):
-        return rg.at[pl.ds(core * (NX * NZ) + ((x + g) % NX) * NZ, NZ)]
-
-    for dz in range(1, NZ):
-        slot = rg.at[core * (NX * NZ) + x * NZ + (zl + dz) % NZ]
-        r_x += [
-            send(slot, slot, rs.at[3 * dz + 2 + dx], rr.at[3 * dz + 2 + dx], dev(dx=dx))
-            for dx in (2, 1, 3)
-        ]
-    r_core = [send(group(0), group(0), rs.at[15], rr.at[15], dev(fc=1))]
 
     for copy in cy + cy2:
         copy.wait_recv()
@@ -205,7 +206,6 @@
         ]
 
     t_core = [chunk(k) for k in range(CH)]
-    t_1 = [after_core(0)]
 
     total = ms[...]
     for i, copy in enumerate(m_x):
@@ -216,7 +216,7 @@
         send(mt, mb.at[i], mss.at[7 + i], mrs.at[7 + i], dev(dz=dz, fz=fz))
         for i, (dz, fz) in enumerate(zz)
     ]
-    t_1 += [after_core(k) for k in range(1, CH)]
+    t_1 = [after_core(k) for k in range(CH)]
 
     for copy in r_x:
         copy.wait_recv()

time: 35.9 us -> 35.2 us (0.981)
  Pallas kernels: 35.2 us -> 34.5 us
    pallas_call x1, Pallas kernels: 33.1 us -> 32.4 us  [body(): pl.pallas_call(kernel, out_shape=[vmem(shape, F32) for shape in SHAPES],...]
where the time goes in v4:
time: 35.2 us; the launch traced here: 35.1 us
  Pallas kernels  34.5 us (98%)
  between operations  0.64 us (2%)
    pallas_call x1, Pallas kernels, body(): pl.pallas_call(kernel, out_shape=[vmem(shape, F32) for shape in SHAPES],...  32.4 us
    pallas_call x1, Pallas kernels, body(): pl.pallas_call(store, out_shape=[jax.ShapeDtypeStruct(shape, F32) for sha...  2.11 us

profile of v4, /device:TPU:1, one launch (start us, length us, event | category | flops | bytes accessed | tf_op | source)
XLA Modules:
  0.0 35.1 jit_solution(3123447512461387141)
XLA Ops:
  0.6 32.4 %block_step.1 = (f32[16,512]{1,0:T(8,128)S(1)}, f32[512,2048]{1,0:T(8,128)S(1)}, f32[4,16]{1,0:T(4,128)S(1)}, f32[4,2048]{1,0:T(4,128)S(1)}) custom-call(f32[16,512]{1,0:T(8,128)} %bitcast.3, f32[16,512]{1,0:T(8,128)} %bitcast.4, f32[128,128]{1,0:T(8,128)} %l_hbm.1, f32[128,128]{1,0:T(8,128)} %d_hbm.1, f32[4,2048]{1,0:T(4,128)} %r_hbm.1, ...), custom_call_target="tpu_custom_call" | custom-call | tf_op jit(solution)/shard_map/block_step/pallas_call | solution.py:367
  33.0 2.1 %store.1 = (f32[16,512]{1,0:T(8,128)}, f32[512,2048]{1,0:T(8,128)}, f32[4,16]{1,0:T(4,128)}, f32[4,2048]{1,0:T(4,128)}) custom-call(f32[16,512]{1,0:T(8,128)S(1)} %get-tuple-element.12.cbar_v, f32[512,2048]{1,0:T(8,128)S(1)} %get-tuple-element.13.bbar_v, f32[4,16]{1,0:T(4,128)S(1)} %get-tuple-element.14.kda_v, f32[4,2048]{1,0:T(4,128)S(1)} %get-tuple-element.15.rbar_v), custom_call_target="tpu_custom_call" | custom-call | tf_op jit(solution)/shard_map/store/pallas_call | solution.py:379

commit v5 on v4

--- a/solution.py
+++ b/solution.py
@@ -12,7 +12,9 @@
 NX, NZ, NY, NC, NH = 4, 4, 4, 2, 2
 CH = 4
 CW = 512
-ZK = 3
+CUTS = (0, 512, 1536, 2048)
+NK = 3
+ZK = 2
 
 
 def dot(a, b, contract=((1,), (0,)), precision=HI):
@@ -180,16 +182,19 @@
     both = jnp.concatenate([nh, nl], axis=0)
 
     def chunk(k):
-        where = slice(k * CW, (k + 1) * CW)
+        where, n = slice(CUTS[k], CUTS[k + 1]), CUTS[k + 1] - CUTS[k]
         p = dot(both, bh_v[:, where], precision=None)
         t = p[:128] + p[128:] + dot(nh, bl_v[:, where], precision=None)
-        tb[k, 0] = t[:64]
-        tb[k, 1] = t[64:]
-        return send(tb.at[k, 1 - core], tc.at[k], tss.at[k], trs.at[k], dev(fc=1))
+        tb[k, 0, :, :n] = t[:64]
+        tb[k, 1, :, :n] = t[64:]
+        w = pl.ds(0, n)
+        return send(tb.at[k, 1 - core, :, w], tc.at[k, :, w], tss.at[k], trs.at[k], dev(fc=1))
 
     def after_core(k):
         t_core[k].wait_recv()
-        v = tb[k, core] + tc[k]
+        n = CUTS[k + 1] - CUTS[k]
+        w = pl.ds(0, n)
+        v = tb[k, core, :, :n] + tc[k, :, :n]
         if k == ZK:
             for q in range(NX):
                 for p in range(NZ):
@@ -199,13 +204,16 @@
                 for dz in range(1, NZ)
             ]
         for q in range(NX):
-            ts[k, q] = v[16 * q : 16 * (q + 1)]
+            ts[k, q, :, :n] = v[16 * q : 16 * (q + 1)]
         return [
-            send(ts.at[k, (x + dx) % NX], xr.at[k, dx - 1], xss.at[k, dx - 1], xrs.at[k, dx - 1], dev(dx=dx))
+            send(
+                ts.at[k, (x + dx) % NX, :, w], xr.at[k, dx - 1, :, w],
+                xss.at[k, dx - 1], xrs.at[k, dx - 1], dev(dx=dx),
+            )
             for dx in (2, 1, 3)
         ]
 
-    t_core = [chunk(k) for k in range(CH)]
+    t_core = [chunk(k) for k in range(NK)]
 
     total = ms[...]
     for i, copy in enumerate(m_x):
@@ -216,7 +224,7 @@
         send(mt, mb.at[i], mss.at[7 + i], mrs.at[7 + i], dev(dz=dz, fz=fz))
         for i, (dz, fz) in enumerate(zz)
     ]
-    t_1 = [after_core(k) for k in range(CH)]
+    t_1 = [after_core(k) for k in range(NK)]
 
     for copy in r_x:
         copy.wait_recv()
@@ -267,15 +275,20 @@
                 send(x1.at[(x + dx) % NX], xr1.at[dx - 1], xss.at[k, dx - 1], xrs.at[k, dx - 1], dev(dx=dx))
                 for dx in (2, 1, 3)
             ]
-        v = ts[k, x] + xr[k, 0] + xr[k, 1] + xr[k, 2]
+        n = CUTS[k + 1] - CUTS[k]
+        w = pl.ds(0, n)
+        v = ts[k, x, :, :n] + xr[k, 0, :, :n] + xr[k, 1, :, :n] + xr[k, 2, :, :n]
         for q in range(NZ):
-            zs[k, q] = v[4 * q : 4 * q + 4]
+            zs[k, q, :, :n] = v[4 * q : 4 * q + 4]
         return [
-            send(zs.at[k, (zl + dz) % NZ], zr.at[k, dz - 1], zss.at[k, dz - 1], zrs.at[k, dz - 1], dev(dz=dz))
+            send(
+                zs.at[k, (zl + dz) % NZ, :, w], zr.at[k, dz - 1, :, w],
+                zss.at[k, dz - 1], zrs.at[k, dz - 1], dev(dz=dz),
+            )
             for dz in range(1, NZ)
         ]
 
-    t_2 = {k: second_axis(k) for k in (0, 1, ZK, 2)}
+    t_2 = {k: second_axis(k) for k in (0, ZK, 1)}
 
     for copy in m_y:
         copy.wait_recv()
@@ -308,14 +321,14 @@
         where = slice(k * CW, (k + 1) * CW)
         corr = dot(a3, r3(k), precision=None)
         rbar_v[:, where] = rbar_v[:, where] - jnp.where(core == 0, corr[:4], corr[4:])
-    for k in range(CH):
-        where = slice(k * CW, (k + 1) * CW)
+    for k in range(NK):
+        where, n = slice(CUTS[k], CUTS[k + 1]), CUTS[k + 1] - CUTS[k]
         for copy in t_2[k]:
             copy.wait_recv()
         if k == ZK:
             acc = x1[x] + xr1[0] + xr1[1] + xr1[2]
         else:
-            acc = zs[k, zl] + zr[k, 0] + zr[k, 1] + zr[k, 2]
+            acc = zs[k, zl, :, :n] + zr[k, 0, :, :n] + zr[k, 1, :, :n] + zr[k, 2, :, :n]
         rbar_out[:, where] = rbar_v[:, where] - acc
     end()
 
@@ -351,9 +364,9 @@
         vmem((128, 128), F32), vmem((128, 128), F32), vmem((128, 128), F32),
         vmem((128, 128), F32), vmem((128, 128), F32),
         vmem((512, 384), BF16), vmem((128, 2048), BF16), vmem((128, 2048), BF16),
-        vmem((CH, 2, 64, CW), F32), vmem((CH, 64, CW), F32), vmem((CH, NX, 16, CW), F32),
-        vmem((CH, NX - 1, 16, CW), F32),
-        vmem((CH, NZ, 4, CW), F32), vmem((CH, NZ - 1, 4, CW), F32),
+        vmem((NK, 2, 64, 1024), F32), vmem((NK, 64, 1024), F32), vmem((NK, NX, 16, 1024), F32),
+        vmem((NK, NX - 1, 16, 1024), F32),
+        vmem((NK, NZ, 4, 1024), F32), vmem((NK, NZ - 1, 4, 1024), F32),
         vmem((NZ, NX, 4, CW), F32), vmem((NZ - 1, NX, 4, CW), F32),
         vmem((NX, 4, CW), F32), vmem((NX - 1, 4, CW), F32),
         vmem((16, 128), F32), vmem((7, 16, 128), F32), vmem((16, 128), F32), vmem((7, 16, 128), F32),

time: 35.2 us -> 35.5 us (level)
  no operation moved by 1% of the time
where the time goes in v5:
time: 35.5 us; the launch traced here: 35.4 us
  Pallas kernels  34.7 us (98%)
  between operations  0.64 us (2%)
    pallas_call x1, Pallas kernels, body(): pl.pallas_call(kernel, out_shape=[vmem(shape, F32) for shape in SHAPES],...  32.6 us
    pallas_call x1, Pallas kernels, body(): pl.pallas_call(store, out_shape=[jax.ShapeDtypeStruct(shape, F32) for sha...  2.11 us

profile of v5, /device:TPU:1, one launch (start us, length us, event | category | flops | bytes accessed | tf_op | source)
XLA Modules:
  0.0 35.4 jit_solution(4119429523083146515)
XLA Ops:
  0.6 32.6 %block_step.1 = (f32[16,512]{1,0:T(8,128)S(1)}, f32[512,2048]{1,0:T(8,128)S(1)}, f32[4,16]{1,0:T(4,128)S(1)}, f32[4,2048]{1,0:T(4,128)S(1)}) custom-call(f32[16,512]{1,0:T(8,128)} %bitcast.3, f32[16,512]{1,0:T(8,128)} %bitcast.4, f32[128,128]{1,0:T(8,128)} %l_hbm.1, f32[128,128]{1,0:T(8,128)} %d_hbm.1, f32[4,2048]{1,0:T(4,128)} %r_hbm.1, ...), custom_call_target="tpu_custom_call" | custom-call | tf_op jit(solution)/shard_map/block_step/pallas_call | solution.py:380
  33.3 2.1 %store.1 = (f32[16,512]{1,0:T(8,128)}, f32[512,2048]{1,0:T(8,128)}, f32[4,16]{1,0:T(4,128)}, f32[4,2048]{1,0:T(4,128)}) custom-call(f32[16,512]{1,0:T(8,128)S(1)} %get-tuple-element.12.cbar_v, f32[512,2048]{1,0:T(8,128)S(1)} %get-tuple-element.13.bbar_v, f32[4,16]{1,0:T(4,128)S(1)} %get-tuple-element.14.kda_v, f32[4,2048]{1,0:T(4,128)S(1)} %get-tuple-element.15.rbar_v), custom_call_target="tpu_custom_call" | custom-call | tf_op jit(solution)/shard_map/store/pallas_call | solution.py:392

commit v6 on v5

--- a/solution.py
+++ b/solution.py
@@ -12,7 +12,7 @@
 NX, NZ, NY, NC, NH = 4, 4, 4, 2, 2
 CH = 4
 CW = 512
-CUTS = (0, 512, 1536, 2048)
+CUTS = (0, 768, 1536, 2048)
 NK = 3
 ZK = 2
 

time: 35.5 us -> 35.4 us (level)
  no operation moved by 1% of the time
where the time goes in v6:
time: 35.4 us; the launch traced here: 35.3 us
  Pallas kernels  34.6 us (98%)
  between operations  0.64 us (2%)
    pallas_call x1, Pallas kernels, body(): pl.pallas_call(kernel, out_shape=[vmem(shape, F32) for shape in SHAPES],...  32.5 us
    pallas_call x1, Pallas kernels, body(): pl.pallas_call(store, out_shape=[jax.ShapeDtypeStruct(shape, F32) for sha...  2.11 us

profile of v6, /device:TPU:1, one launch (start us, length us, event | category | flops | bytes accessed | tf_op | source)
XLA Modules:
  0.0 35.3 jit_solution(1585471187665937253)
XLA Ops:
  0.6 32.5 %block_step.1 = (f32[16,512]{1,0:T(8,128)S(1)}, f32[512,2048]{1,0:T(8,128)S(1)}, f32[4,16]{1,0:T(4,128)S(1)}, f32[4,2048]{1,0:T(4,128)S(1)}) custom-call(f32[16,512]{1,0:T(8,128)} %bitcast.3, f32[16,512]{1,0:T(8,128)} %bitcast.4, f32[128,128]{1,0:T(8,128)} %l_hbm.1, f32[128,128]{1,0:T(8,128)} %d_hbm.1, f32[4,2048]{1,0:T(4,128)} %r_hbm.1, ...), custom_call_target="tpu_custom_call" | custom-call | tf_op jit(solution)/shard_map/block_step/pallas_call | solution.py:380
  33.2 2.1 %store.1 = (f32[16,512]{1,0:T(8,128)}, f32[512,2048]{1,0:T(8,128)}, f32[4,16]{1,0:T(4,128)}, f32[4,2048]{1,0:T(4,128)}) custom-call(f32[16,512]{1,0:T(8,128)S(1)} %get-tuple-element.12.cbar_v, f32[512,2048]{1,0:T(8,128)S(1)} %get-tuple-element.13.bbar_v, f32[4,16]{1,0:T(4,128)S(1)} %get-tuple-element.14.kda_v, f32[4,2048]{1,0:T(4,128)S(1)} %get-tuple-element.15.rbar_v), custom_call_target="tpu_custom_call" | custom-call | tf_op jit(solution)/shard_map/store/pallas_call | solution.py:392
